TPU v7x, 32 devices: a whole 2x2x4 slice. The times are simulated.
32 devices in a mesh: fsdp: 4 (over y, x), heads: 4 (over z), tensor: 2 (over core).
Axes of the slice: x: 2, y: 2, z: 4, core: 2. Of those that a mesh axis runs over, the one named last changes fastest.
Arguments:
- tokens: bfloat16 [12608, 512], P(('fsdp', 'heads', 'tensor')), may hold values from -6 to 6
- cotangent: bfloat16 [12608, 512], P(('fsdp', 'heads', 'tensor')), may hold values from -6 to 6
- image_counts: int32 [4], P('fsdp'), may hold values from 15 to 16
- w_qkv: bfloat16 [1, 3, 512, 512], P(None, None, 'fsdp', ('heads', 'tensor')), may hold values from -0.25 to 0.25
- w_out: bfloat16 [1, 512, 512], P(None, ('heads', 'tensor'), 'fsdp'), may hold values from -1 to 1
- ln_gain: float32 [1, 2, 512], replicated, may hold values from 0.5 to 1.5
- ln_bias: float32 [1, 2, 512], replicated, may hold values from -1.75 to 1.75
- w_router: bfloat16 [1, 512, 32], replicated, may hold values from -0.1875 to 0.1875
- w_in: bfloat16 [1, 32, 512, 2048], P(None, 'heads', 'fsdp', 'tensor'), may hold values from -0.25 to 0.25
- w_back: bfloat16 [1, 32, 2048, 512], P(None, 'heads', 'tensor', 'fsdp'), may hold values from -2 to 2
- expert_ids: int32 [1, 12608, 2], P(None, 'fsdp'), may hold values from 0 to 31, as said below
- slots: int32 [1, 12608, 2], P(None, 'fsdp'), may hold values from -1 to 255, as said below
Outputs:
- output: bfloat16 [12608, 512], P(('fsdp', 'heads', 'tensor'))
- tokens_grad: float32 [12608, 512], P(('fsdp', 'heads', 'tensor'))
- w_qkv_grad: float32 [1, 3, 512, 512], P(None, None, 'fsdp', ('heads', 'tensor'))
- w_out_grad: float32 [1, 512, 512], P(None, ('heads', 'tensor'), 'fsdp')
- ln_gain_grad: float32 [1, 2, 512], replicated
- ln_bias_grad: float32 [1, 2, 512], replicated
- w_router_grad: float32 [1, 512, 32], replicated
- w_in_grad: float32 [1, 32, 512, 2048], P(None, 'heads', 'fsdp', 'tensor')
- w_back_grad: float32 [1, 32, 2048, 512], P(None, 'heads', 'tensor', 'fsdp')
Inputs may be any that keep to these rules, and one draw needn't show every extreme that they name: `expert_ids`: each token names two different experts. `slots`: a choice's slot is its place, in token order, among the choices of its group and block that name the same expert, or -1 where that place is 256 or more; in every group and block some expert is named more than 256 times.
All inputs are finite; a program needn't handle non-finite values.
Results may differ from a plain program's by a relative error of at most 0.012.
Values may be sent and summed in bfloat16 or wider, within the bound.
A program may use at most 192 MiB of HBM per device.

v0:
```python
import jax
import jax.numpy as jnp
from jax import lax
from jax.sharding import PartitionSpec as P

HEAD = 64
SEQ = 197
LAYERS = 1
CAP = 256


def layer_norm(value, ln_gains, ln_shift):
    centred = value - jnp.mean(value, axis=-1, keepdims=True)
    spread = jnp.mean(centred * centred, axis=-1, keepdims=True)
    return centred * lax.rsqrt(spread + 1e-06) * ln_gains + ln_shift


def gelu_exact(value):
    return jax.nn.gelu(value, approximate=False)


def with_zero_row(matrix):
    return jnp.concatenate([matrix, jnp.zeros((1,) + matrix.shape[1:], matrix.dtype)], axis=0)


def slot_tables(named_expert, slot_rows, first_expert, local_experts):
    group_rows = named_expert.shape[0]
    is_local = (
        (slot_rows >= 0)
        & (named_expert >= first_expert)
        & (named_expert < first_expert + local_experts)
    )
    places = jnp.where(
        is_local, (named_expert - first_expert) * CAP + slot_rows, local_experts * CAP
    )
    picked = jnp.full((local_experts * CAP + 1,), 2 * group_rows, jnp.int32)
    picked = picked.at[places.reshape(-1)].set(jnp.arange(2 * group_rows, dtype=jnp.int32))
    return (places, picked[: local_experts * CAP])


def joined_qkv(qkv_weight):
    head_cols = qkv_weight.shape[2]
    return jnp.transpose(qkv_weight, (1, 0, 2)).reshape(qkv_weight.shape[1], 3 * head_cols)


def forward_block(
    residual, weights, ln_gains, ln_shift, router_weight, named_expert, slot_rows, first_expert
):
    qkv_weight, out_weight, in_weight, back_weight = weights
    own_rows, widths = residual.shape
    group_rows = named_expert.shape[0]
    head_cols = qkv_weight.shape[2]
    local_experts = in_weight.shape[0]
    head_shape = (group_rows // SEQ, SEQ, head_cols // HEAD, HEAD)
    q_scale = HEAD ** (-0.5)
    flat_qkv = joined_qkv(qkv_weight)
    normed_rows = layer_norm(residual, ln_gains[0], ln_shift[0]).astype(jnp.bfloat16)
    normed = lax.all_gather(normed_rows, ("heads", "tensor"), axis=0, tiled=True)
    projected = jnp.dot(normed, flat_qkv, preferred_element_type=jnp.float32)
    queries = (projected[:, :head_cols] * q_scale).astype(jnp.bfloat16).reshape(head_shape)
    key_rows = projected[:, head_cols : 2 * head_cols].astype(jnp.bfloat16).reshape(head_shape)
    value_rows = projected[:, 2 * head_cols :].astype(jnp.bfloat16).reshape(head_shape)
    scores = jnp.einsum("bqhd,bkhd->bhqk", queries, key_rows, preferred_element_type=jnp.float32)
    log_total = jax.nn.logsumexp(scores, axis=-1)
    attn_probs = jax.nn.softmax(scores, axis=-1).astype(jnp.bfloat16)
    mixed_rows = jnp.einsum(
        "bhqk,bkhd->bqhd", attn_probs, value_rows, preferred_element_type=jnp.float32
    )
    mixed_rows = mixed_rows.reshape(group_rows, head_cols).astype(jnp.bfloat16)
    middle = residual + lax.psum_scatter(
        jnp.dot(mixed_rows, out_weight, preferred_element_type=jnp.float32),
        ("heads", "tensor"),
        scatter_dimension=0,
        tiled=True,
    )
    head_full = ()
    normed_two_rows = layer_norm(middle, ln_gains[1], ln_shift[1]).astype(jnp.bfloat16)
    normed_two = lax.all_gather(normed_two_rows, ("heads", "tensor"), axis=0, tiled=True)
    router = jax.nn.softmax(
        jnp.dot(normed_two, router_weight, preferred_element_type=jnp.float32), axis=-1
    )
    gate_values = jnp.take_along_axis(router, named_expert, axis=1) * (slot_rows >= 0)
    places, picked = slot_tables(named_expert, slot_rows, first_expert, local_experts)
    routed = with_zero_row(normed_two)[picked // 2].reshape(local_experts, CAP, widths)
    hidden = jnp.einsum("ecd,edf->ecf", routed, in_weight, preferred_element_type=jnp.float32)
    active = gelu_exact(hidden).astype(jnp.bfloat16)
    result = jnp.einsum("ecf,efd->ecd", active, back_weight, preferred_element_type=jnp.float32)
    flat_result = with_zero_row(result.reshape(local_experts * CAP, widths))
    block_out = middle + lax.psum_scatter(
        (
            flat_result[places[:, 0]] * gate_values[:, 0:1]
            + flat_result[places[:, 1]] * gate_values[:, 1:2]
        ).astype(jnp.bfloat16),
        ("heads", "tensor"),
        scatter_dimension=0,
        tiled=True,
    ).astype(jnp.float32)
    stored = (
        residual,
        middle,
        normed,
        queries,
        key_rows,
        value_rows,
        log_total,
        mixed_rows,
        normed_two_rows,
        router,
        gate_values,
        places,
        picked,
        routed,
        hidden,
        active,
        flat_result,
    )
    return (block_out, stored, head_full)


def backward_block(
    grad_rows, stored, weights, ln_gains, ln_shift, router_weight, named_expert, row_start
):
    qkv_weight, out_weight, in_weight, back_weight = weights
    (
        residual,
        middle,
        normed,
        queries,
        key_rows,
        value_rows,
        log_total,
        mixed_rows,
        normed_two_rows,
        router,
        gate_values,
        places,
        picked,
        routed,
        hidden,
        active,
        flat_result,
    ) = stored
    own_rows, widths = residual.shape
    group_rows = named_expert.shape[0]
    head_cols = qkv_weight.shape[2]
    local_experts = in_weight.shape[0]
    expert_count = router.shape[1]
    q_scale = HEAD ** (-0.5)
    flat_qkv = joined_qkv(qkv_weight)
    grad_moe = lax.all_gather(
        grad_rows.astype(jnp.bfloat16), ("heads", "tensor"), axis=0, tiled=True
    )
    back_rows = with_zero_row(grad_moe)[picked // 2].astype(jnp.float32)
    gate_slots = with_zero_row(gate_values.reshape(-1))[picked]
    gate_grad_slots = jnp.sum(back_rows * flat_result[:-1], axis=1)
    gate_grads = with_zero_row(gate_grad_slots)[places]
    expert_range = jnp.arange(expert_count, dtype=jnp.int32)
    router_part = jnp.sum(
        gate_grads[:, :, None]
        * (named_expert[:, :, None] == expert_range[None, None, :]).astype(jnp.float32),
        axis=1,
    )
    grad_result = (
        (gate_slots[:, None] * back_rows).astype(jnp.bfloat16).reshape(local_experts, CAP, widths)
    )
    grad_active = jnp.einsum(
        "ecd,efd->ecf", grad_result, back_weight, preferred_element_type=jnp.float32
    )
    gelu_value, gelu_pull = jax.vjp(gelu_exact, hidden)
    grad_hidden = gelu_pull(grad_active)[0].astype(jnp.bfloat16)
    back_grad = jnp.einsum("ecf,ecd->efd", active, grad_result, preferred_element_type=jnp.float32)
    in_grad = jnp.einsum("ecd,ecf->edf", routed, grad_hidden, preferred_element_type=jnp.float32)
    grad_routed = jnp.einsum(
        "ecf,edf->ecd", grad_hidden, in_weight, preferred_element_type=jnp.float32
    )
    grad_routed = with_zero_row(grad_routed.reshape(local_experts * CAP, widths))
    token_part = grad_routed[places[:, 0]] + grad_routed[places[:, 1]]
    grad_normed_two, router_rows = (
        lax.psum_scatter(token_part, ("heads", "tensor"), scatter_dimension=0, tiled=True),
        lax.psum_scatter(router_part, ("heads", "tensor"), scatter_dimension=0, tiled=True),
    )
    router_own = lax.dynamic_slice_in_dim(router, row_start, own_rows, 0)
    grad_logits = (
        router_own * (router_rows - jnp.sum(router_own * router_rows, axis=-1, keepdims=True))
    ).astype(jnp.bfloat16)
    router_grad = jnp.einsum(
        "td,te->de", normed_two_rows, grad_logits, preferred_element_type=jnp.float32
    )
    grad_normed_two = grad_normed_two + jnp.einsum(
        "te,de->td", grad_logits, router_weight, preferred_element_type=jnp.float32
    )
    norm_value, norm_pull = jax.vjp(layer_norm, middle, ln_gains[1], ln_shift[1])
    grad_middle, gain_two, shift_two = norm_pull(grad_normed_two)
    grad_middle = grad_middle + grad_rows
    grad_attn = lax.all_gather(
        grad_middle.astype(jnp.bfloat16), ("heads", "tensor"), axis=0, tiled=True
    )
    out_grad = jnp.einsum("tc,td->cd", mixed_rows, grad_attn, preferred_element_type=jnp.float32)
    grad_mixed = jnp.einsum("td,cd->tc", grad_attn, out_weight, preferred_element_type=jnp.float32)
    grad_mixed = grad_mixed.astype(jnp.bfloat16).reshape(queries.shape)
    scores = jnp.einsum("bqhd,bkhd->bhqk", queries, key_rows, preferred_element_type=jnp.float32)
    attn_probs = jnp.exp(scores - log_total[..., None])
    grad_values = jnp.einsum(
        "bhqk,bqhd->bkhd",
        attn_probs.astype(jnp.bfloat16),
        grad_mixed,
        preferred_element_type=jnp.float32,
    )
    grad_probs = jnp.einsum(
        "bqhd,bkhd->bhqk", grad_mixed, value_rows, preferred_element_type=jnp.float32
    )
    grad_scores = (
        attn_probs * (grad_probs - jnp.sum(attn_probs * grad_probs, axis=-1, keepdims=True))
    ).astype(jnp.bfloat16)
    grad_queries = jnp.einsum(
        "bhqk,bkhd->bqhd", grad_scores, key_rows, preferred_element_type=jnp.float32
    )
    grad_keys = jnp.einsum(
        "bhqk,bqhd->bkhd", grad_scores, queries, preferred_element_type=jnp.float32
    )
    grad_projected = jnp.concatenate(
        [
            grad_queries.reshape(group_rows, head_cols),
            grad_keys.reshape(group_rows, head_cols),
            grad_values.reshape(group_rows, head_cols),
        ],
        axis=1,
    ).astype(jnp.bfloat16)
    qkv_flat_grad = jnp.einsum(
        "td,tc->dc", normed, grad_projected, preferred_element_type=jnp.float32
    )
    column_scale = jnp.concatenate(
        [jnp.full((head_cols,), q_scale, jnp.float32), jnp.ones((2 * head_cols,), jnp.float32)]
    )
    qkv_grad = jnp.transpose(
        (qkv_flat_grad * column_scale).reshape(widths, 3, head_cols), (1, 0, 2)
    )
    query_term = (
        jnp.einsum(
            "tc,dc->td",
            grad_projected[:, :head_cols],
            flat_qkv[:, :head_cols],
            preferred_element_type=jnp.float32,
        )
        * q_scale
    )
    grad_normed = lax.psum_scatter(
        query_term
        + jnp.einsum(
            "tc,dc->td",
            grad_projected[:, head_cols:],
            flat_qkv[:, head_cols:],
            preferred_element_type=jnp.float32,
        ),
        ("heads", "tensor"),
        scatter_dimension=0,
        tiled=True,
    )
    first_value, first_pull = jax.vjp(layer_norm, residual, ln_gains[0], ln_shift[0])
    grad_input, gain_one, shift_one = first_pull(grad_normed)
    grad_input = grad_input + grad_middle
    matrix_grads = (qkv_grad, out_grad, in_grad, back_grad)
    small_grads = (jnp.stack([gain_one, gain_two]), jnp.stack([shift_one, shift_two]), router_grad)
    return (grad_input, matrix_grads, small_grads)


def on_device(
    tokens,
    cotangent,
    image_counts,
    w_qkv,
    w_out,
    ln_gain,
    ln_bias,
    w_router,
    w_in,
    w_back,
    expert_ids,
    slots,
):
    own_rows = tokens.shape[0]
    row_start = lax.axis_index(("heads", "tensor")) * own_rows
    first_expert = lax.axis_index("heads") * w_in.shape[1]
    residual = tokens.astype(jnp.float32)
    head_list = []
    block_index = 0
    weights = (
        lax.all_gather(w_qkv[block_index], "fsdp", axis=1, tiled=True),
        lax.all_gather(w_out[block_index], "fsdp", axis=1, tiled=True),
        lax.all_gather(w_in[block_index], "fsdp", axis=1, tiled=True),
        lax.all_gather(w_back[block_index], "fsdp", axis=2, tiled=True),
    )
    residual, stored, head_full = forward_block(
        residual,
        weights,
        ln_gain[block_index],
        ln_bias[block_index],
        w_router[block_index],
        expert_ids[block_index],
        slots[block_index],
        first_expert,
    )
    stored_list = [stored]
    head_list.append(head_full)
    image_index = (row_start + jnp.arange(own_rows, dtype=jnp.int32)) // SEQ
    live_rows = (image_index < image_counts[0]).astype(jnp.float32)
    grad_rows = cotangent.astype(jnp.float32) * live_rows[:, None]
    matrix_list = [None] * LAYERS
    small_list = [None] * LAYERS
    for block_index in reversed(range(LAYERS)):
        weights = (
            lax.all_gather(w_qkv[block_index], "fsdp", axis=1, tiled=True),
            lax.all_gather(w_out[block_index], "fsdp", axis=1, tiled=True),
            lax.all_gather(w_in[block_index], "fsdp", axis=1, tiled=True),
            lax.all_gather(w_back[block_index], "fsdp", axis=2, tiled=True),
        )
        grad_rows, matrix_grads, small_grads = backward_block(
            grad_rows,
            stored_list[block_index],
            weights,
            ln_gain[block_index],
            ln_bias[block_index],
            w_router[block_index],
            expert_ids[block_index],
            row_start,
        )
        matrix_list[block_index] = (
            lax.psum_scatter(matrix_grads[0], "fsdp", scatter_dimension=1, tiled=True),
            lax.psum_scatter(matrix_grads[1], "fsdp", scatter_dimension=1, tiled=True),
            lax.psum_scatter(matrix_grads[2], "fsdp", scatter_dimension=1, tiled=True),
            lax.psum_scatter(matrix_grads[3], "fsdp", scatter_dimension=2, tiled=True),
        )
        small_list[block_index] = small_grads
    gain_grads, shift_grads, router_grads = lax.psum(
        (
            jnp.stack([entry[0] for entry in small_list]),
            jnp.stack([entry[1] for entry in small_list]),
            jnp.stack([entry[2] for entry in small_list]),
        ),
        ("fsdp", "heads", "tensor"),
    )
    qkv_grads = jnp.stack([entry[0] for entry in matrix_list])
    out_grads = jnp.stack([entry[1] for entry in matrix_list])
    in_grads = jnp.stack([entry[2] for entry in matrix_list])
    back_grads = jnp.stack([entry[3] for entry in matrix_list])
    return (
        residual.astype(jnp.bfloat16),
        grad_rows,
        qkv_grads,
        out_grads,
        gain_grads,
        shift_grads,
        router_grads,
        in_grads,
        back_grads,
    )


def solution(mesh):
    return jax.shard_map(
        on_device,
        mesh=mesh,
        in_specs=(
            P(("fsdp", "heads", "tensor"), None),
            P(("fsdp", "heads", "tensor"), None),
            P("fsdp"),
            P(None, None, "fsdp", ("heads", "tensor")),
            P(None, ("heads", "tensor"), "fsdp"),
            P(),
            P(),
            P(),
            P(None, "heads", "fsdp", "tensor"),
            P(None, "heads", "tensor", "fsdp"),
            P(None, "fsdp", None),
            P(None, "fsdp", None),
        ),
        out_specs=(
            P(("fsdp", "heads", "tensor"), None),
            P(("fsdp", "heads", "tensor"), None),
            P(None, None, "fsdp", ("heads", "tensor")),
            P(None, ("heads", "tensor"), "fsdp"),
            P(),
            P(),
            P(),
            P(None, "heads", "fsdp", "tensor"),
            P(None, "heads", "tensor", "fsdp"),
        ),
        check_vma=False,
    )
```

profile of v0, /device:TPU:0, one launch (start us, length us, event | category | flops | bytes accessed | tf_op | source)
XLA Modules:
  0.0 1186.9 jit_solution(2514989493225500097)
XLA Ops:
  17.1 9.8 all-gather.1
  35.5 20.6 %all-gather.19.cloned.1.call-done = bf16[8,394,512]{2,1,0:T(8,128)(2,1)} async-done(((bf16[1,394,512]{2,1,0:T(8,128)(2,1)}), bf16[8,394,512]{2,1,0:T(8,128)(2,1)}) %all-gather.19.cloned.1.call-update) | async-done | bytes 3227664 | tf_op jit(solution)/shard_map/all_gather | solution.py:58
  76.1 80.6 %fusion = f32[400,512]{1,0:T(8,128)S(1)} fusion(f32[3152,512]{1,0:T(8,128)} %fusion.90), kind=kCustom, calls=%all-reduce-scatter | all-reduce-scatter fusion | flops 1638401 | bytes 7275008
  183.8 29.9 %scatter_custom_fusion = s32[2049]{0:T(1024)S(1)} fusion(s32[6304]{0:T(1024)S(1)} %fusion.98, s32[6304]{0:T(1024)S(1)} %iota.12, s32[]{:T(128)} %constant.64.clone.1), kind=kCustom, calls=%fused_computation.183 | custom fusion | bytes 8200 | tf_op jit(solution)/shard_map/scatter | solution.py:37
  238.1 9.2 gather_fusion
  250.4 48.5 %gather_fusion.8 = f32[6304]{0:T(1024)S(1)} fusion(f32[3152,32]{0,1:T(8,128)S(1)} %fusion.85, s32[6304]{0:T(1024)S(1)} %reshape.533), kind=kCustom, calls=%fused_computation.8 | custom fusion | bytes 100864 | tf_op jit(solution)/shard_map/jit(take_along_axis)/gather | solution.py:82
  301.8 11.8 gather_fusion.3
  328.3 19.8 %multiply_convert_fusion = (bf16[8,256,1024]{2,1,0:T(8,128)(2,1)}, f32[8,256,1024]{2,1,0:T(8,128)}) fusion(f32[8,256,1024]{2,1,0:T(8,128)S(1)} %get-tuple-element.48, u8[256,1024]{1,0:T(8,128)(4,1)S(1)} %get-tuple-element.10, u8[256,1024]{1,0:T(8,128)(4,1)S(1)} %get-tuple-element.9), kind=kLoop, calls=%fused_computation.26 | loop fusion | flops 146800640 | bytes 21495808 | tf_op jit(solution)/shard_map/convert_element_type | solution.py:86
  348.0 33.0 %all-gather.17.cloned.1.call-done = bf16[1,8,1024,512]{3,2,1,0:T(8,128)(2,1)} async-done(((bf16[1,8,1024,128]{3,2,1,0:T(8,128)(2,1)}), bf16[1,8,1024,512]{3,2,1,0:T(8,128)(2,1)}) %all-gather.17.cloned.1.call-update) | async-done | bytes 8388624 | tf_op jit(solution)/shard_map/all_gather | solution.py:291
  381.0 13.8 %add_convert_fusion = bf16[8,256,1024]{2,1,0:T(8,128)(2,1)} fusion(f32[8,256,1024]{2,1,0:T(8,128)} %get-tuple-element.28, f32[8,256,1024]{2,1,0:T(8,128)} %copy-done.20, bf16[1,8,1024,512]{3,2,1,0:T(8,128)(2,1)} %all-gather.17.cloned.1.call-done, bf16[8,256,512]{2,1,0:T(8,128)(2,1)S(1)} %bitcast.180, f32[8,256]{1,0:T(8,128)S(1)} %mul.311), kind=kOutput, calls=%fused_computation.25 | convolution fusion | flops 2179989504 | bytes 31465472 | tf_op jit(solution)/shard_map/ecd,efd->ecf/dot_general | solution.py:166
  410.6 13.1 %gather_fusion.2 = f32[3152,512]{1,0:T(8,128)} fusion(f32[2049,512]{1,0:T(8,128)} %concatenate.26, s32[4096]{0:T(1024)S(1)} %copy-done.41), kind=kCustom, calls=%fused_computation.2 | custom fusion | bytes 12923200 | tf_op jit(solution)/shard_map/gather | solution.py:92
  423.7 13.1 %gather_fusion.1 = f32[3152,512]{1,0:T(8,128)} fusion(f32[2049,512]{1,0:T(8,128)} %concatenate.26, s32[4096]{0:T(1024)S(1)} %copy-done.42), kind=kCustom, calls=%fused_computation.1 | custom fusion | bytes 12923200 | tf_op jit(solution)/shard_map/gather | solution.py:91
  436.8 13.0 %gather_fusion.5 = f32[3152,512]{1,0:T(8,128)} fusion(f32[2049,512]{1,0:T(8,128)} %concatenate.29, s32[4096]{0:T(1024)S(1)} %copy-done.42), kind=kCustom, calls=%fused_computation.5 | custom fusion | bytes 12923200 | tf_op jit(solution)/shard_map/gather | solution.py:177
  449.8 13.1 %gather_fusion.6 = f32[3152,512]{1,0:T(8,128)} fusion(f32[2049,512]{1,0:T(8,128)} %concatenate.29, s32[4096]{0:T(1024)S(1)} %copy-done.41), kind=kCustom, calls=%fused_computation.6 | custom fusion | bytes 12923200 | tf_op jit(solution)/shard_map/gather | solution.py:177
  462.9 33.1 %gather_fusion.7 = f32[6304]{0:T(1024)S(1)} fusion(f32[2049]{0:T(1024)S(1)} %pad_maximum_fusion.1, s32[7168]{0:T(1024)S(1)} %copy-done.2), kind=kCustom, calls=%fused_computation.7 | custom fusion | bytes 75648 | tf_op jit(solution)/shard_map/gather | solution.py:156
  508.1 75.9 %fusion.2 = f32[400,512]{1,0:T(8,128)S(1)} fusion(f32[3152,512]{1,0:T(8,128)} %add.261), kind=kCustom, calls=%all-reduce-scatter.2 | all-reduce-scatter fusion | flops 1638401 | bytes 7275008
  592.2 39.7 %fusion.1 = bf16[400,512]{1,0:T(8,128)(2,1)S(1)} fusion(bf16[3152,512]{1,0:T(8,128)(2,1)} %add_convert_fusion.1), kind=kCustom, calls=%all-reduce-scatter.1 | all-reduce-scatter fusion | flops 1638401 | bytes 3637760
  645.8 37.2 %all-gather.25.cloned.1.call-done = bf16[8,394,512]{2,1,0:T(8,128)(2,1)} async-done(((bf16[1,394,512]{2,1,0:T(8,128)(2,1)}), bf16[8,394,512]{2,1,0:T(8,128)(2,1)}) %all-gather.25.cloned.1.call-update) | async-done | bytes 3227664 | tf_op jit(solution)/shard_map/all_gather | solution.py:195
  708.7 10.6 fusion.26
  720.8 10.3 fusion.128
  736.8 70.5 %fusion.3 = f32[400,512]{1,0:T(8,128)S(1)} fusion(f32[3152,512]{1,0:T(8,128)} %convolution_add_fusion), kind=kCustom, calls=%all-reduce-scatter.3 | all-reduce-scatter fusion | flops 1638401 | bytes 7275008
  811.8 42.5 %all-reduce.13 = (f32[1,2,512]{2,1,0:T(2,128)}, f32[1,2,512]{2,1,0:T(2,128)}) all-reduce(f32[1,2,512]{2,1,0:T(2,128)S(1)} %maximum_bitcast_fusion, f32[1,2,512]{2,1,0:T(2,128)S(1)} %maximum_bitcast_fusion.1), channel_id=1, replica_groups=mesh['fsdp'=4,'heads'=4,'tensor'=2] {'fsdp','heads','tensor'}, use_global_device_ids=true, to_apply=%region_27.28 | all-reduce | flops 2048 | bytes 16384 | tf_op jit(solution)/shard_map/psum | solution.py:334
  863.3 157.5 %reduce-scatter.20.cloned.1.call-done = f32[8,1024,128]{2,1,0:T(8,128)} async-done(((f32[8,1024,512]{2,1,0:T(8,128)}), f32[8,1024,128]{2,1,0:T(8,128)}) %reduce-scatter.20.cloned.1.call-update) | async-done | bytes 4194320 | tf_op jit(solution)/shard_map/reduce_scatter | solution.py:331
  1020.8 157.4 %reduce-scatter.18.cloned.1.call-done = f32[8,128,1024]{2,1,0:T(8,128)} async-done(((f32[8,512,1024]{2,1,0:T(8,128)}), f32[8,128,1024]{2,1,0:T(8,128)}) %reduce-scatter.18.cloned.1.call-update) | async-done | bytes 4194320 | tf_op jit(solution)/shard_map/reduce_scatter | solution.py:330
  (305 shorter events, 205.5 us)
Async XLA Ops:
  7.2 240.1 %copy-start = (bf16[1,512,32]{1,2,0:T(8,128)(2,1)S(1)}, bf16[1,512,32]{1,2,0:T(8,128)(2,1)}, u32[]{:S(2)}) copy-start(bf16[1,512,32]{1,2,0:T(8,128)(2,1)} %param.19) | copy-start | bytes 98308
  7.2 48.9 %all-gather.19.cloned.1.call-start = ((), (), s32[]{:S(2)}) async-start(), calls=%async_computation.11 | async-start | bytes 3686400 | tf_op jit(solution)/shard_map/all_gather | solution.py:58
  11.0 150.0 %copy-start.56 = (f32[1,1,512]{2,1,0:T(1,128)}, f32[1,1,512]{2,1,0:T(1,128)S(1)}, u32[]{:S(2)}) copy-start(f32[1,1,512]{2,1,0:T(1,128)S(1)} %get-tuple-element.38) | copy-start | bytes 6148
  11.8 149.3 %copy-start.66 = (f32[1,1,512]{2,1,0:T(1,128)}, f32[1,1,512]{2,1,0:T(1,128)S(1)}, u32[]{:S(2)}) copy-start(f32[1,1,512]{2,1,0:T(1,128)S(1)} %get-tuple-element.40) | copy-start | bytes 6148
  13.8 203.6 %all-gather.23.cloned.1.call-start = ((), (), s32[]{:S(2)}) async-start(), calls=%async_computation.13 | async-start | bytes 3686400 | tf_op jit(solution)/shard_map/all_gather | solution.py:150
  17.1 215.3 %all-gather.21.cloned.1.call-start = ((), (), s32[]{:S(2)}) async-start(), calls=%async_computation.12 | async-start | bytes 3686400 | tf_op jit(solution)/shard_map/all_gather | solution.py:78
  76.1 81.9 %copy-start.71 = (u32[32]{0:T(128)S(1)}, u32[32]{0:T(128)}, u32[]{:S(2)}) copy-start(u32[32]{0:T(128)} %constant.194) | copy-start | bytes 388
  76.1 84.4 %copy-start.14 = (bf16[394,512]{1,0:T(8,128)(2,1)S(1)}, bf16[394,512]{1,0:T(8,128)(2,1)}, u32[]{:S(2)}) copy-start(bf16[394,512]{1,0:T(8,128)(2,1)} %param.12) | copy-start | bytes 1210372
  156.7 2.6 collective-permute-start
  162.6 154.8 %all-gather.15.cloned.1.call-start = ((), (), s32[]{:S(2)}) async-start(), calls=%async_computation.9 | async-start | bytes 10485760 | tf_op jit(solution)/shard_map/all_gather | solution.py:290
  163.2 217.8 %all-gather.17.cloned.1.call-start = ((), (), s32[]{:S(2)}) async-start(), calls=%async_computation.10 | async-start | bytes 10485760 | tf_op jit(solution)/shard_map/all_gather | solution.py:291
  163.8 472.8 %all-reduce.19.cloned.1.call-start = ((), (), s32[]{:S(2)}) async-start(), calls=%async_computation.15 | async-start | bytes 819200
  499.0 184.0 %all-gather.25.cloned.1.call-start = ((), (), s32[]{:S(2)}) async-start(), calls=%async_computation.14 | async-start | bytes 3686400 | tf_op jit(solution)/shard_map/all_gather | solution.py:195
  508.1 77.2 %copy-start.50 = (f32[3152]{0:T(1024)S(1)}, f32[3152]{0:T(1024)}, u32[]{:S(2)}) copy-start(f32[3152]{0:T(1024)} %get-tuple-element.16) | copy-start | bytes 37828
  584.0 51.2 %collective-permute-start.2 = (f32[42,512]{1,0:T(8,128)S(1)}, f32[42,512]{1,0:T(8,128)S(1)}, u32[]{:S(2)}, u32[]{:S(2)}) collective-permute-start(f32[42,512]{1,0:T(8,128)S(1)} %slice.99), channel_id=1, source_target_pairs={{0,1},{1,2},{2,3},{3,4},{4,5},{5,6},{6,7},{8,9},{9,10},{10,11},{11... | collective-permute-start | bytes 258056
  631.8 2.2 collective-permute-start.1
  643.7 212.0 %all-reduce.17.cloned.1.call-start = ((), (), s32[]{:S(2)}) async-start(), calls=%async_computation.6 | async-start | bytes 131072 | tf_op jit(solution)/shard_map/psum | solution.py:334
  645.8 209.9 %reduce-scatter.16.cloned.1.call-start = ((), (), s32[]{:S(2)}) async-start(), calls=%async_computation.5 | async-start | bytes 163840 | tf_op jit(solution)/shard_map/reduce_scatter | solution.py:329
  704.9 158.5 %reduce-scatter.14.cloned.1.call-start = ((), (), s32[]{:S(2)}) async-start(), calls=%async_computation.4 | async-start | bytes 491520 | tf_op jit(solution)/shard_map/reduce_scatter | solution.py:328
  708.6 312.2 %reduce-scatter.20.cloned.1.call-start = ((), (), s32[]{:S(2)}) async-start(), calls=%async_computation.8 | async-start | bytes 20971520 | tf_op jit(solution)/shard_map/reduce_scatter | solution.py:331
  719.3 458.9 %reduce-scatter.18.cloned.1.call-start = ((), (), s32[]{:S(2)}) async-start(), calls=%async_computation.7 | async-start | bytes 20971520 | tf_op jit(solution)/shard_map/reduce_scatter | solution.py:330
  736.8 117.5 %copy-start.22 = (f32[394,512]{1,0:T(8,128)S(1)}, f32[394,512]{1,0:T(8,128)}, u32[]{:S(2)}) copy-start(f32[394,512]{1,0:T(8,128)} %copy-done.21) | copy-start | bytes 2420740
  736.8 117.5 %copy-start.30 = (bf16[394,512]{1,0:T(8,128)(2,1)S(1)}, bf16[394,512]{1,0:T(8,128)(2,1)}, u32[]{:S(2)}) copy-start(bf16[394,512]{1,0:T(8,128)(2,1)} %param.13) | copy-start | bytes 1210372
  807.4 2.2 collective-permute-start.3
  (65 other events, 1263.8 us)
Sparse Core Ops, SparseCore 0:
  14.0 42.0 all-gather.18
  57.7 43.8 all-gather.22
  162.8 40.8 all-gather.20
  205.3 86.4 all-gather.14
  293.5 87.4 all-gather.16
  499.2 57.1 all-reduce.18
  643.8 39.1 all-gather.24
  689.5 118.1 all-reduce.16
  811.3 24.3 reduce-scatter.15
  838.9 24.4 reduce-scatter.13
  867.0 153.7 reduce-scatter.19
  1024.3 153.8 reduce-scatter.17
where the time goes:
time: 1200 us; the launch traced here: 1190 us
  waiting for transfers between devices  416 us (35%)
  blocking collectives  328 us (27%)
  local copies, waits for them, and re-layouts  274 us (23%)
  matrix products  84.7 us (7%)
  other arithmetic  60.9 us (5%)
  between operations  17.8 us (1%)
    unnamed x4, blocking collectives  267 us
    reduce_scatter x1, waiting for transfers between devices, on_device(): lax.psum_scatter(matrix_grads[3], 'fsdp', scatter_dimension=2, tiled=True)  157 us
    reduce_scatter x1, waiting for transfers between devices, on_device(): lax.psum_scatter(matrix_grads[2], 'fsdp', scatter_dimension=1, tiled=True)  157 us
    gather x4, local copies, waits for them, and re-layouts, forward_block(): jnp.take_along_axis(router, named_expert, axis=1) * (slot_rows >= 0)  55.1 us
    psum x1, blocking collectives, on_device(): lax.psum((jnp.stack([entry[0] for entry in small_list]), jnp.stack([entry...  42.5 us
    all_gather x1, waiting for transfers between devices, backward_block(): lax.all_gather(grad_middle.astype(jnp.bfloat16), ('heads', 'tensor'), axi...  37.2 us
    gather x3, local copies, waits for them, and re-layouts, backward_block(): gate_grads = with_zero_row(gate_grad_slots)[places]  35.2 us
    all_gather x1, waiting for transfers between devices, on_device(): lax.all_gather(w_back[block_index], 'fsdp', axis=2, tiled=True)  33 us
  transfers between devices with their start and end apart: 16, of which 8 were waited for; matrix products, arithmetic and copies ran while one was open for 46% of the time, Pallas kernels for 0%

commit v1 on v0

--- a/solution.py
+++ b/solution.py
@@ -355,8 +355,190 @@
         back_grads,
     )
 
+def fast_device(
+    tokens,
+    cotangent,
+    image_counts,
+    w_qkv,
+    w_out,
+    ln_gain,
+    ln_bias,
+    w_router,
+    w_in,
+    w_back,
+    expert_ids,
+    slots,
+):
+    group_axes = ("heads", "tensor")
+    own_rows, widths = tokens.shape
+    images = own_rows // SEQ
+    own_group = lax.axis_size("fsdp")
+    cores = lax.axis_size("tensor")
+    core = lax.axis_index("tensor")
+    heads_index = lax.axis_index("heads")
+    local_experts = w_in.shape[1]
+    my_expert = heads_index * local_experts + lax.axis_index("fsdp") * cores + core
+    row_start = lax.axis_index(group_axes) * own_rows
+    q_scale = HEAD ** (-0.5)
+    f32, bf16 = jnp.float32, jnp.bfloat16
+
+    qkv_full = lax.all_gather(w_qkv[0], "fsdp", axis=1, tiled=True)
+    qkv_full = lax.all_gather(qkv_full, group_axes, axis=2, tiled=True)
+    out_full = lax.all_gather(w_out[0], "fsdp", axis=1, tiled=True)
+    out_full = lax.all_gather(out_full, group_axes, axis=0, tiled=True)
+    flat_qkv = joined_qkv(qkv_full)
+
+    def to_expert(weight):
+        return lax.all_to_all(weight, ("fsdp", "tensor"), 0, 0, tiled=True)
+
+    def from_expert(blocks):
+        return lax.all_to_all(blocks, ("fsdp", "tensor"), 0, 0, tiled=True)
+
+    depth, width = w_in.shape[2], w_in.shape[3]
+    in_blocks = to_expert(w_in[0]).reshape(own_group, cores, depth, width)
+    in_full = jnp.transpose(in_blocks, (0, 2, 1, 3)).reshape(own_group * depth, cores * width)
+    back_blocks = to_expert(w_back[0]).reshape(own_group, cores, width, depth)
+    back_full = jnp.transpose(back_blocks, (1, 2, 0, 3)).reshape(cores * width, own_group * depth)
+
+    image_index = (row_start + jnp.arange(own_rows, dtype=jnp.int32)) // SEQ
+    live_rows = (image_index < image_counts[0]).astype(f32)
+    grad_rows = cotangent.astype(f32) * live_rows[:, None]
+    grad_all = lax.all_gather(grad_rows.astype(bf16), group_axes, axis=0, tiled=True)
+
+    relative = expert_ids[0] - heads_index * local_experts
+    wanted = (
+        (slots[0] >= 0) & (relative >= 0) & (relative < local_experts) & (relative % cores == core)
+    )
+    places = jnp.where(wanted, (relative // cores) * CAP + slots[0], -1)
+    slot_range = jnp.arange(own_group * CAP, dtype=jnp.int32)[None, :]
+    chosen = (
+        (places[:, 0:1] == slot_range) | (places[:, 1:2] == slot_range)
+    ).astype(bf16)
+
+    def dispatch(rows):
+        picked = jnp.einsum("ts,td->sd", chosen, rows, preferred_element_type=f32).astype(bf16)
+        return lax.all_to_all(picked, "fsdp", 0, 0, tiled=True)
+
+    def combine(rows):
+        back = lax.all_to_all(rows, "fsdp", 0, 0, tiled=True)
+        part = jnp.einsum("ts,sd->td", chosen, back, preferred_element_type=f32).astype(bf16)
+        return lax.psum_scatter(part, group_axes, scatter_dimension=0, tiled=True).astype(f32)
+
+    routed_grad = dispatch(grad_all)
+
+    residual = tokens.astype(f32)
+    head_shape = (images, SEQ, widths // HEAD, HEAD)
+    normed = layer_norm(residual, ln_gain[0, 0], ln_bias[0, 0]).astype(bf16)
+    projected = jnp.dot(normed, flat_qkv, preferred_element_type=f32)
+    queries = (projected[:, :widths] * q_scale).astype(bf16).reshape(head_shape)
+    key_rows = projected[:, widths : 2 * widths].astype(bf16).reshape(head_shape)
+    value_rows = projected[:, 2 * widths :].astype(bf16).reshape(head_shape)
+    scores = jnp.einsum("bqhd,bkhd->bhqk", queries, key_rows, preferred_element_type=f32)
+    attn_probs = jax.nn.softmax(scores, axis=-1)
+    probs_low = attn_probs.astype(bf16)
+    mixed_rows = jnp.einsum("bhqk,bkhd->bqhd", probs_low, value_rows, preferred_element_type=f32)
+    mixed_rows = mixed_rows.reshape(own_rows, widths).astype(bf16)
+    middle = residual + jnp.dot(mixed_rows, out_full, preferred_element_type=f32)
+    normed_two = layer_norm(middle, ln_gain[0, 1], ln_bias[0, 1]).astype(bf16)
+
+    routed = dispatch(lax.all_gather(normed_two, group_axes, axis=0, tiled=True))
+
+    router = jax.nn.softmax(jnp.dot(routed, w_router[0], preferred_element_type=f32), axis=-1)
+    mine = (jnp.arange(router.shape[1], dtype=jnp.int32) == my_expert).astype(f32)[None, :]
+    gates = jnp.sum(router * mine, axis=1, keepdims=True)
+    hidden = jnp.dot(routed, in_full, preferred_element_type=f32)
+    gelu_value, gelu_pull = jax.vjp(gelu_exact, hidden)
+    active = gelu_value.astype(bf16)
+    result = jnp.dot(active, back_full, preferred_element_type=f32)
+    gate_grads = jnp.sum(routed_grad.astype(f32) * result, axis=1, keepdims=True)
+    grad_result = (gates * routed_grad.astype(f32)).astype(bf16)
+    grad_active = jnp.einsum("cd,fd->cf", grad_result, back_full, preferred_element_type=f32)
+    grad_hidden = gelu_pull(grad_active)[0].astype(bf16)
+    grad_logits = (gate_grads * gates * (mine - router)).astype(bf16)
+    grad_routed = jnp.einsum("cf,df->cd", grad_hidden, in_full, preferred_element_type=f32)
+    grad_routed += jnp.einsum("ce,de->cd", grad_logits, w_router[0], preferred_element_type=f32)
+    grad_normed_two = combine(grad_routed.astype(bf16))
+    block_out = middle + combine((gates * result).astype(bf16))
+
+    back_grad = jnp.einsum("cf,cd->fd", active, grad_result, preferred_element_type=f32).astype(bf16)
+    in_grad = jnp.einsum("cd,cf->df", routed, grad_hidden, preferred_element_type=f32).astype(bf16)
+    router_grad = jnp.einsum("cd,ce->de", routed, grad_logits, preferred_element_type=f32)
+    in_parts = jnp.transpose(in_grad.reshape(own_group, depth, cores, width), (0, 2, 1, 3))
+    in_grads = from_expert(in_parts.reshape(w_in.shape[1:])).astype(f32)
+    back_parts = jnp.transpose(back_grad.reshape(cores, width, own_group, depth), (2, 0, 1, 3))
+    back_grads = from_expert(back_parts.reshape(w_back.shape[1:])).astype(f32)
+
+    norm_value, norm_pull = jax.vjp(layer_norm, middle, ln_gain[0, 1], ln_bias[0, 1])
+    grad_middle, gain_two, shift_two = norm_pull(grad_normed_two)
+    grad_middle = grad_middle + grad_rows
+    grad_attn = grad_middle.astype(bf16)
+    out_grad = jnp.einsum("tc,td->cd", mixed_rows, grad_attn, preferred_element_type=f32)
+    grad_mixed = jnp.einsum("td,cd->tc", grad_attn, out_full, preferred_element_type=f32)
+    grad_mixed = grad_mixed.astype(bf16).reshape(head_shape)
+    grad_values = jnp.einsum("bhqk,bqhd->bkhd", probs_low, grad_mixed, preferred_element_type=f32)
+    grad_probs = jnp.einsum("bqhd,bkhd->bhqk", grad_mixed, value_rows, preferred_element_type=f32)
+    grad_scores = (
+        attn_probs * (grad_probs - jnp.sum(attn_probs * grad_probs, axis=-1, keepdims=True))
+    ).astype(bf16)
+    grad_queries = jnp.einsum("bhqk,bkhd->bqhd", grad_scores, key_rows, preferred_element_type=f32)
+    grad_keys = jnp.einsum("bhqk,bqhd->bkhd", grad_scores, queries, preferred_element_type=f32)
+    grad_projected = jnp.concatenate(
+        [
+            grad_queries.reshape(own_rows, widths) * q_scale,
+            grad_keys.reshape(own_rows, widths),
+            grad_values.reshape(own_rows, widths),
+        ],
+        axis=1,
+    ).astype(bf16)
+    qkv_grad = jnp.einsum("td,tc->dc", normed, grad_projected, preferred_element_type=f32)
+    qkv_grad = jnp.transpose(qkv_grad.reshape(widths, 3, widths), (1, 0, 2))
+    grad_normed = jnp.einsum("tc,dc->td", grad_projected, flat_qkv, preferred_element_type=f32)
+    first_value, first_pull = jax.vjp(layer_norm, residual, ln_gain[0, 0], ln_bias[0, 0])
+    grad_input, gain_one, shift_one = first_pull(grad_normed)
+    grad_input = grad_input + grad_middle
+
+    qkv_grads = lax.psum_scatter(
+        qkv_grad.astype(bf16), group_axes, scatter_dimension=2, tiled=True
+    )
+    qkv_grads = lax.psum_scatter(qkv_grads, "fsdp", scatter_dimension=1, tiled=True)
+    out_grads = lax.psum_scatter(
+        out_grad.astype(bf16), group_axes, scatter_dimension=0, tiled=True
+    )
+    out_grads = lax.psum_scatter(out_grads, "fsdp", scatter_dimension=1, tiled=True)
+    gain_grads, shift_grads, router_grads = lax.psum(
+        (
+            jnp.stack([gain_one, gain_two])[None],
+            jnp.stack([shift_one, shift_two])[None],
+            router_grad[None],
+        ),
+        ("fsdp", "heads", "tensor"),
+    )
+    return (
+        block_out.astype(bf16),
+        grad_input,
+        qkv_grads.astype(f32)[None],
+        out_grads.astype(f32)[None],
+        gain_grads,
+        shift_grads,
+        router_grads,
+        in_grads[None],
+        back_grads[None],
+    )
+
 
 def solution(mesh):
+    def program(*arrays):
+        sizes = dict(mesh.shape)
+        planes = sizes["fsdp"] * sizes["tensor"]
+        own_rows = arrays[0].shape[0] // (planes * sizes["heads"])
+        experts = arrays[8].shape[1] // sizes["heads"]
+        own_expert = experts == planes and own_rows % SEQ == 0
+        return placed(mesh, fast_device if own_expert else on_device)(*arrays)
+
+    return program
+
+
+def placed(mesh, on_device):
     return jax.shard_map(
         on_device,
         mesh=mesh,

time: 1200 us -> 606 us (0.51)
  waiting for transfers between devices: 416 us -> 139 us
  local copies, waits for them, and re-layouts: 274 us -> 74.7 us
  blocking collectives: 328 us -> 192 us
  other arithmetic: 60.9 us -> 28.1 us
  starting transfers between devices: 6.09 us -> 34.2 us
  matrix products: 84.7 us -> 112 us
    reduce_scatter x4 -> x2, waiting for transfers between devices: 322 us -> 20.5 us  [the longest x1 20.5 us: fast_device(): lax.psum_scatter(qkv_grad.astype(bf16), group_axes, scatter_dimension=2,...]
    unnamed x4 -> x1, blocking collectives: 267 us -> 69.9 us
    gather x14 -> x0, local copies, waits for them, and re-layouts: 173 us -> none  [the longest x4 55.1 us: forward_block(): jnp.take_along_axis(router, named_expert, axis=1) * (slot_rows >= 0)]
    all_gather x6 -> x3, waiting for transfers between devices: 90.8 us -> 0.01 us  [the longest x1 0.01 us: fast_device(): qkv_full = lax.all_gather(qkv_full, group_axes, axis=2, tiled=True)]
    psum x1, waiting for transfers between devices: 0.01 us -> 87.1 us  [fast_device(): lax.psum((jnp.stack([gain_one, gain_two])[None], jnp.stack([shift_one, sh...]
    all_to_all x0 -> x7, waiting for transfers between devices: none -> 31.2 us  [the longest x1 20.6 us: to_expert(): return lax.all_to_all(weight, ('fsdp', 'tensor'), 0, 0, tiled=True)]
    all_to_all x0 -> x1, blocking collectives: none -> 31 us  [to_expert(): return lax.all_to_all(weight, ('fsdp', 'tensor'), 0, 0, tiled=True)]
    all_to_all x0 -> x7, starting transfers between devices: none -> 30.3 us  [the longest x2 8.93 us: from_expert(): return lax.all_to_all(blocks, ('fsdp', 'tensor'), 0, 0, tiled=True)]
  transfers between devices with their start and end apart: 16 -> 17, of which waited for: 8 -> 5; matrix products, arithmetic and copies ran while one was open for 46% -> 28% of each run, Pallas kernels for 0% -> 0%
where the time goes in v1:
time: 606 us; the launch traced here: 596 us
  blocking collectives  192 us (32%)
  waiting for transfers between devices  139 us (23%)
  matrix products  112 us (18%)
  local copies, waits for them, and re-layouts  74.7 us (12%)
  starting transfers between devices  34.2 us (6%)
  other arithmetic  28.1 us (5%)
  between operations  16.7 us (3%)
    psum x1, waiting for transfers between devices, fast_device(): lax.psum((jnp.stack([gain_one, gain_two])[None], jnp.stack([shift_one, sh...  87.1 us
    unnamed x1, blocking collectives  69.9 us
    psum x1, blocking collectives, fast_device(): lax.psum((jnp.stack([gain_one, gain_two])[None], jnp.stack([shift_one, sh...  54.8 us
    all_to_all x1, blocking collectives, to_expert(): return lax.all_to_all(weight, ('fsdp', 'tensor'), 0, 0, tiled=True)  31 us
    unnamed x99, local copies, waits for them, and re-layouts  30.6 us
    dot_general x1, matrix products, fast_device(): hidden = jnp.dot(routed, in_full, preferred_element_type=f32)  22.8 us
    all_to_all x1, waiting for transfers between devices, to_expert(): return lax.all_to_all(weight, ('fsdp', 'tensor'), 0, 0, tiled=True)  20.6 us
    reduce_scatter x1, waiting for transfers between devices, fast_device(): lax.psum_scatter(qkv_grad.astype(bf16), group_axes, scatter_dimension=2,...  20.5 us
  transfers between devices with their start and end apart: 17, of which 5 were waited for; matrix products, arithmetic and copies ran while one was open for 28% of the time, Pallas kernels for 0%

profile of v1, /device:TPU:0, one launch (start us, length us, event | category | flops | bytes accessed | tf_op | source)
XLA Modules:
  0.0 596.3 jit_solution(4670882593616123615)
XLA Ops:
  7.2 11.8 %all-gather = bf16[1,3,512,64]{2,3,1,0:T(8,128)(2,1)} all-gather(bf16[1,3,128,64]{2,3,1,0:T(8,128)(2,1)} %param.15), channel_id=2, replica_groups=mesh['fsdp'=4,'heads'=4,'tensor'=2] {'fsdp'}, dimensions={2}, use_global_device_ids=true | all-gather | bytes 245760 | tf_op jit(solution)/shard_map/all_gather | solution.py:385
  22.4 7.4 %all-gather.2 = bf16[1,64,512]{2,1,0:T(8,128)(2,1)S(1)} all-gather(bf16[1,64,128]{2,1,0:T(8,128)(2,1)} %param.16), channel_id=4, replica_groups=mesh['fsdp'=4,'heads'=4,'tensor'=2] {'fsdp'}, dimensions={2}, use_global_device_ids=true | all-gather | bytes 81920 | tf_op jit(solution)/shard_map/all_gather | solution.py:387
  34.3 16.7 %all-gather.3 = bf16[1,512,512]{2,1,0:T(8,128)(2,1)S(1)} all-gather(bf16[1,64,512]{2,1,0:T(8,128)(2,1)S(1)} %all-gather.2), channel_id=5, replica_groups=mesh['fsdp'=4,'heads'=4,'tensor'=2] {'heads','tensor'}, dimensions={1}, use_global_device_ids=true | all-gather | bytes 589824 | tf_op jit(solution)/shard_map/all_gather | solution.py:388
  66.9 31.0 %all_to_all.65 = bf16[8,128,1024]{2,1,0:T(8,128)(2,1)} all-to-all(bf16[8,128,1024]{2,1,0:T(8,128)(2,1)} %bitcast.186), channel_id=1, replica_groups=mesh['fsdp'=4,'heads'=4,'tensor'=2] {'fsdp','tensor'}, dimensions={0} | all-to-all | bytes 4194304 | tf_op jit(solution)/shard_map/all_to_all | solution.py:392
  97.9 4.6 all-to-all-start.2
  108.5 20.6 %all-to-all-done.2 = bf16[8,1024,128]{2,1,0:T(8,128)(2,1)} async-done(((bf16[8,1024,128]{2,1,0:T(8,128)(2,1)}), bf16[8,1024,128]{2,1,0:T(8,128)(2,1)}, u32[]{:S(2)}, u32[]{:S(2)}) %all-to-all-start.2) | async-done | bytes 2097184 | tf_op jit(solution)/shard_map/all_to_all | solution.py:392
  129.1 4.5 copy.70
  140.8 7.5 %fusion.24 = bf16[1024,512]{1,0:T(8,128)(2,1)} fusion(bf16[3152,512]{1,0:T(8,128)(2,1)} %reshape.222, s32[3152]{0:T(1024)S(1)} %get-tuple-element.17, s32[3152]{0:T(1024)S(1)} %get-tuple-element.16), kind=kOutput, calls=%fused_computation.47 | convolution fusion | flops 3315318784 | bytes 4301440 | tf_op jit(solution)/shard_map/ts,td->sd/dot_general | solution.py:419
  152.2 7.5 %fusion.27 = bf16[1024,512]{1,0:T(8,128)(2,1)} fusion(bf16[3152,512]{1,0:T(8,128)(2,1)} %reshape.224, s32[3152]{0:T(1024)S(1)} %get-tuple-element.17, s32[3152]{0:T(1024)S(1)} %get-tuple-element.16), kind=kOutput, calls=%fused_computation.48 | convolution fusion | flops 3315318784 | bytes 4301440 | tf_op jit(solution)/shard_map/ts,td->sd/dot_general | solution.py:419
  159.7 5.3 all-to-all-done
  169.3 22.8 %multiply_convert_fusion = (bf16[1024,2048]{1,0:T(8,128)(2,1)}, f32[1024,2048]{1,0:T(8,128)}, f32[1024,2048]{1,0:T(8,128)}) fusion(bf16[1024,512]{1,0:T(8,128)(2,1)S(1)} %bitcast.172, bf16[512,2048]{1,0:T(8,128)(2,1)} %bitcast.188), kind=kOutput, calls=%fused_computation.7 | convolution fusion | flops 2283798528 | bytes 24117248 | tf_op jit(solution)/shard_map/dot_general | solution.py:449
  192.8 6.8 %fusion.20 = (f32[1024]{0:T(1024)S(1)}, bf16[1024,512]{1,0:T(8,128)(2,1)}, bf16[1024,512]{1,0:T(8,128)(2,1)}) fusion(bf16[4,256,512]{2,1,0:T(8,128)(2,1)} %all-to-all-done.4, f32[1024]{0:T(1024)S(1)} %multiply_reduce_fusion.2, bf16[1024,2048]{1,0:T(8,128)(2,1)} %get-tuple-element.26, bf16[256,8,4,128]{3,2,1,0:T(4,128)(2,1)} %bitcast.190), kind=kOutput, calls=%fused_computation.40 | convolution fusion | flops 2151152640 | bytes 9445376 | tf_op jit(solution)/shard_map/dot_general | solution.py:452
  205.6 9.0 %add_convert_fusion = bf16[1024,2048]{1,0:T(8,128)(2,1)S(1)} fusion(f32[1024,2048]{1,0:T(8,128)} %get-tuple-element.27, f32[1024,2048]{1,0:T(8,128)} %get-tuple-element.44, bf16[1024,512]{1,0:T(8,128)(2,1)S(1)} %bitcast.196, bf16[256,8,4,128]{3,2,1,0:T(4,128)(2,1)} %bitcast.191), kind=kOutput, calls=%fused_computation.6 | convolution fusion | flops 2176843776 | bytes 24117248 | tf_op jit(solution)/shard_map/cd,fd->cf/dot_general | solution.py:455
  222.8 7.1 %convolution_convert_fusion.1 = bf16[3152,512]{1,0:T(8,128)(2,1)} fusion(bf16[1024,512]{1,0:T(8,128)(2,1)} %bitcast.22, s32[3152]{0:T(1024)S(1)} %get-tuple-element.17, s32[3152]{0:T(1024)S(1)} %get-tuple-element.16), kind=kOutput, calls=%fused_computation.22 | convolution fusion | flops 3316408320 | bytes 4301440 | tf_op jit(solution)/shard_map/ts,sd->td/dot_general | solution.py:424
  229.9 5.2 all-to-all-done.5
  235.2 7.1 %convolution_convert_fusion = bf16[3152,512]{1,0:T(8,128)(2,1)} fusion(bf16[1024,512]{1,0:T(8,128)(2,1)} %bitcast.29, s32[3152]{0:T(1024)S(1)} %get-tuple-element.17, s32[3152]{0:T(1024)S(1)} %get-tuple-element.16), kind=kOutput, calls=%fused_computation.21 | convolution fusion | flops 3316408320 | bytes 4301440 | tf_op jit(solution)/shard_map/ts,sd->td/dot_general | solution.py:424
  242.3 69.9 %fusion.76 = (bf16[400,512]{1,0:T(8,128)(2,1)}, bf16[400,512]{1,0:T(8,128)(2,1)}) fusion(bf16[3152,512]{1,0:T(8,128)(2,1)} %convolution_convert_fusion.1, bf16[3152,512]{1,0:T(8,128)(2,1)} %convolution_convert_fusion), kind=kCustom, calls=%all-reduce-scatter.2 | all-reduce-scatter fusion | flops 3276801 | bytes 7275008
  367.7 6.2 %convolution_convert_fusion.2 = bf16[2048,512]{1,0:T(8,128)(2,1)} fusion(bf16[1024,2048]{1,0:T(8,128)(2,1)} %get-tuple-element.26, bf16[1024,512]{1,0:T(8,128)(2,1)} %get-tuple-element.32), kind=kOutput, calls=%fused_computation.28 | convolution fusion | flops 2148532224 | bytes 7340032 | tf_op jit(solution)/shard_map/cf,cd->fd/dot_general | solution.py:463
  381.1 4.6 all-to-all-start.7
  387.4 20.5 %reduce-scatter.13.cloned.1.call-done = bf16[3,512,64]{1,2,0:T(8,128)(2,1)} async-done(((bf16[3,512,512]{1,2,0:T(8,128)(2,1)}), bf16[3,512,64]{1,2,0:T(8,128)(2,1)}) %reduce-scatter.13.cloned.1.call-update) | async-done | bytes 196624 | tf_op jit(solution)/shard_map/reduce_scatter | solution.py:500
  410.2 5.9 convolution_convert_fusion.3
  416.1 4.5 reshape.208
  433.1 54.8 %all-reduce.4 = (f32[1,2,512]{2,1,0:T(2,128)}, f32[1,2,512]{2,1,0:T(2,128)}) all-reduce(f32[1,2,512]{2,1,0:T(2,128)S(1)} %get-tuple-element.50, f32[1,2,512]{2,1,0:T(2,128)S(1)} %get-tuple-element.51), channel_id=1, replica_groups=mesh['fsdp'=4,'heads'=4,'tensor'=2] {'fsdp','heads','tensor'}, use_global_device_ids=true, to_apply=%region_23.24 | all-reduce | flops 2048 | bytes 16384 | tf_op jit(solution)/shard_map/psum | solution.py:508
  500.4 87.1 %all-reduce.8.cloned.1.call-done = f32[1,512,32]{1,2,0:T(8,128)} async-done(((f32[1,512,32]{1,2,0:T(8,128)}), f32[1,512,32]{1,2,0:T(8,128)}) %all-reduce.8.cloned.1.call-update) | async-done | bytes 65552 | tf_op jit(solution)/shard_map/psum | solution.py:508
  (209 shorter events, 151.0 us)
Async XLA Ops:
  7.2 185.0 %copy-start = (bf16[1,512,32]{1,2,0:T(8,128)(2,1)S(1)}, bf16[1,512,32]{1,2,0:T(8,128)(2,1)}, u32[]{:S(2)}) copy-start(bf16[1,512,32]{1,2,0:T(8,128)(2,1)} %param.19) | copy-start | bytes 98308
  7.2 43.7 %copy-start.1 = (bf16[394,512]{1,0:T(8,128)(2,1)S(1)}, bf16[394,512]{1,0:T(8,128)(2,1)}, u32[]{:S(2)}) copy-start(bf16[394,512]{1,0:T(8,128)(2,1)} %param.12) | copy-start | bytes 1210372
  7.2 43.7 %all-gather.10.cloned.1.call-start = ((), (), s32[]{:S(2)}) async-start(), calls=%async_computation.15 | async-start | bytes 1769472 | tf_op jit(solution)/shard_map/all_gather | solution.py:386
  19.1 114.6 %all-gather.14.cloned.1.call-start = ((), (), s32[]{:S(2)}) async-start(), calls=%async_computation.17 | async-start | bytes 3686400 | tf_op jit(solution)/shard_map/all_gather | solution.py:406
  22.3 114.9 %all-gather.12.cloned.1.call-start = ((), (), s32[]{:S(2)}) async-start(), calls=%async_computation.16 | async-start | bytes 3686400 | tf_op jit(solution)/shard_map/all_gather | solution.py:444
  66.9 35.6 %copy-start.29 = (s32[1,3152,2]{1,2,0:T(2,128)S(1)}, s32[1,3152,2]{1,2,0:T(2,128)}, u32[]{:S(2)}) copy-start(s32[1,3152,2]{1,2,0:T(2,128)} %param.23) | copy-start | bytes 75652
  97.9 31.2 %all-to-all-start.2 = ((bf16[8,1024,128]{2,1,0:T(8,128)(2,1)}), bf16[8,1024,128]{2,1,0:T(8,128)(2,1)}, u32[]{:S(2)}, u32[]{:S(2)}) async-start(bf16[8,1024,128]{2,1,0:T(8,128)(2,1)} %bitcast.187), calls=%async_computation.2 | async-start | bytes 4194304 | tf_op jit(solution)/shard_map/all_to_all | solution.py:392
  102.5 114.5 %copy-start.37 = (f32[32]{0:T(128)}, f32[32]{0:T(128)S(1)}, u32[]{:S(2)}) copy-start(f32[32]{0:T(128)S(1)} %compare_convert_fusion) | copy-start | bytes 388
  148.3 16.8 %all-to-all-start = ((bf16[4,256,512]{2,1,0:T(8,128)(2,1)}), bf16[4,256,512]{2,1,0:T(8,128)(2,1)S(1)}, u32[]{:S(2)}, u32[]{:S(2)}) async-start(bf16[4,256,512]{2,1,0:T(8,128)(2,1)} %bitcast.195), calls=%async_computation | async-start | bytes 2097152 | tf_op jit(solution)/shard_map/all_to_all | solution.py:420
  165.1 27.7 %all-to-all-start.4 = ((bf16[4,256,512]{2,1,0:T(8,128)(2,1)}), bf16[4,256,512]{2,1,0:T(8,128)(2,1)}, u32[]{:S(2)}, u32[]{:S(2)}) async-start(bf16[4,256,512]{2,1,0:T(8,128)(2,1)} %bitcast.194), calls=%async_computation.4 | async-start | bytes 2097152 | tf_op jit(solution)/shard_map/all_to_all | solution.py:420
  199.6 18.9 %all-to-all-start.3 = ((bf16[4,256,512]{2,1,0:T(8,128)(2,1)}), bf16[4,256,512]{2,1,0:T(8,128)(2,1)}, u32[]{:S(2)}, u32[]{:S(2)}) async-start(bf16[4,256,512]{2,1,0:T(8,128)(2,1)} %bitcast.193), calls=%async_computation.3 | async-start | bytes 2097152 | tf_op jit(solution)/shard_map/all_to_all | solution.py:423
  218.5 16.6 %all-to-all-start.5 = ((bf16[4,256,512]{2,1,0:T(8,128)(2,1)}), bf16[4,256,512]{2,1,0:T(8,128)(2,1)}, u32[]{:S(2)}, u32[]{:S(2)}) async-start(bf16[4,256,512]{2,1,0:T(8,128)(2,1)} %bitcast.185), calls=%async_computation.5 | async-start | bytes 2097152 | tf_op jit(solution)/shard_map/all_to_all | solution.py:423
  222.8 162.9 %reduce-scatter.15.cloned.1.call-start = ((), (), s32[]{:S(2)}) async-start(), calls=%async_computation.13 | async-start | bytes 589824 | tf_op jit(solution)/shard_map/reduce_scatter | solution.py:504
  242.3 72.1 %copy-start.39 = (u32[32]{0:T(128)S(1)}, u32[32]{0:T(128)}, u32[]{:S(2)}) copy-start(u32[32]{0:T(128)} %constant.142) | copy-start | bytes 388
  313.1 5.6 collective-permute-start.1
  316.4 8.2 %collective-permute-start = (bf16[42,512]{1,0:T(8,128)(2,1)S(1)}, bf16[42,512]{1,0:T(8,128)(2,1)S(1)}, u32[]{:S(2)}, u32[]{:S(2)}) collective-permute-start(bf16[42,512]{1,0:T(8,128)(2,1)S(1)} %slice.45), channel_id=1, source_target_pairs={{0,1},{1,2},{2,3},{3,4},{4,5},{5,6},{6,7},{8,9},{9,10},{10,11},{11... | collective-permute-start | bytes 129032
  343.1 64.8 %reduce-scatter.13.cloned.1.call-start = ((), (), s32[]{:S(2)}) async-start(), calls=%async_computation.12 | async-start | bytes 1769472 | tf_op jit(solution)/shard_map/reduce_scatter | solution.py:500
  381.1 43.1 %all-to-all-start.7 = ((bf16[8,1024,128]{2,1,0:T(8,128)(2,1)}), bf16[8,1024,128]{2,1,0:T(8,128)(2,1)}, u32[]{:S(2)}, u32[]{:S(2)}) async-start(bf16[8,1024,128]{2,1,0:T(8,128)(2,1)} %bitcast.177), calls=%async_computation.9 | async-start | bytes 4194304 | tf_op jit(solution)/shard_map/all_to_all | solution.py:395
  385.6 111.6 %reduce-scatter.19.cloned.1.call-start = ((), (), s32[]{:S(2)}) async-start(), calls=%async_computation.19 | async-start | bytes 163840
  387.3 111.3 %reduce-scatter.17.cloned.1.call-start = ((), (), s32[]{:S(2)}) async-start(), calls=%async_computation.18 | async-start | bytes 327680
  424.2 68.9 %all-to-all-start.6 = ((bf16[8,128,1024]{2,1,0:T(8,128)(2,1)}), bf16[8,128,1024]{2,1,0:T(8,128)(2,1)}, u32[]{:S(2)}, u32[]{:S(2)}) async-start(bf16[8,128,1024]{2,1,0:T(8,128)(2,1)} %bitcast.176), calls=%async_computation.8 | async-start | bytes 4194304 | tf_op jit(solution)/shard_map/all_to_all | solution.py:395
  428.5 159.0 %all-reduce.8.cloned.1.call-start = ((), (), s32[]{:S(2)}) async-start(), calls=%async_computation.14 | async-start | bytes 131072 | tf_op jit(solution)/shard_map/psum | solution.py:508
  429.6 58.3 %copy-start.4 = (f32[394,512]{1,0:T(8,128)S(1)}, f32[394,512]{1,0:T(8,128)}, u32[]{:S(2)}) copy-start(f32[394,512]{1,0:T(8,128)} %copy-done.3) | copy-start | bytes 2420740
  429.6 58.3 %copy-start.26 = (f32[394]{0:T(512)S(1)}, f32[394]{0:T(512)}, u32[]{:S(2)}) copy-start(f32[394]{0:T(512)} %copy-done.24) | copy-start | bytes 4732
  (34 other events, 326.9 us)
Sparse Core Ops, SparseCore 0:
  19.2 28.5 all-gather.9
  50.0 38.6 all-gather.13
  91.0 38.2 all-gather.11
  343.3 29.9 reduce-scatter.14
  375.5 32.3 reduce-scatter.12
  410.7 21.7 reduce-scatter.18
  435.2 27.6 reduce-scatter.16
  470.0 117.5 all-reduce.7
